TPU v7x, 32 devices: a whole 2x2x4 slice. The times are simulated.
32 devices in a mesh: gx: 4 (over y, x), gy: 8 (over z, core).
Axes of the slice: x: 2, y: 2, z: 4, core: 2. Of those that a mesh axis runs over, the one named last changes fastest.
Arguments:
- pulses_in: float32 [12, 64, 128, 256], P(None, 'gx', 'gy'), may hold values from -6 to 6
- node_loss: float32 [64, 128, 256], P('gx', 'gy'), may hold values from 0.5 to 1
- surface_cells: int32 [4, 8, 512], P('gx', 'gy'), may hold values from 0 to 65535
- surface_normal: int32 [4, 8, 512], P('gx', 'gy'), may hold values from 0 to 6, as said below
- owner_dirs: int32 [4096], replicated, may hold values from 0 to 4095, each once
Outputs:
- pulses_out: float32 [12, 64, 128, 256], P(None, 'gx', 'gy')
- far_field: float32 [4096, 96], P(('gx', 'gy'))
Inputs may be any that keep to these rules, and one draw needn't show every extreme that they name: `surface_normal`: on each device the live slots (codes 1 to 6: outward normal +x, -x, +y, -y, +z, -z) come first and the rest are 0; at most 512 are live on a device and some device has all 512 live.
All inputs are finite; a program needn't handle non-finite values.
Results may differ from a plain program's by a relative error of at most 0.0003.
Values sent between devices are 32-bit elements; how exact they have to be, the bound alone decides.
A program may use at most 128 MiB of HBM per device.

v0:
```python
import functools
import math

import jax
import jax.numpy as jnp
import numpy as np
from jax import lax
from jax.experimental import pallas as pl
from jax.experimental.pallas import tpu as pltpu
from jax.sharding import PartitionSpec as P

DIRS = 4096
FREQ = 8


HIGH = lax.Precision.HIGHEST
OTHERS = ((1, 2), (0, 2), (0, 1))


def sums_and_differences(ports):
    total, change = {}, {}
    for arm in range(3):
        for at, polarity in enumerate(OTHERS[arm]):
            plus, minus = ports[4 * arm + at], ports[4 * arm + 2 + at]
            total[arm, polarity] = plus + minus
            change[arm, polarity] = plus - minus
    return total, change


def reflect(total, change, half_loss):
    reflected = [None] * 12
    for arm in range(3):
        for at, polarity in enumerate(OTHERS[arm]):
            third = 3 - arm - polarity
            even = total[third, polarity]
            odd = change[polarity, arm]
            reflected[4 * arm + at] = half_loss * (even - odd)
            reflected[4 * arm + 2 + at] = half_loss * (even + odd)
    return reflected


def node_fields(total, change):
    electric = [
        0.5 * (total[OTHERS[p][0], p] + total[OTHERS[p][1], p]) for p in range(3)
    ]
    magnetic = [
        0.5 * (change[OTHERS[r][0], OTHERS[r][1]] - change[OTHERS[r][1], OTHERS[r][0]])
        for r in range(3)
    ]
    return electric + magnetic


def tlm_kernel(
    size_x, size_y,
    pulses_hbm, loss_hbm, cells_hbm, codes_hbm,
    pulses_out, gat_one, gat_two,
    refl, y_face, y_halo, result, fields, select_z, picked,
    loss, cells, codes, load_sem,
    halo_send, halo_recv, send_z, recv_z, send_x, recv_x, send_c, recv_c, out_sem,
):
    tile_x, tile_y, tile_z = loss.shape
    slots = cells.shape[2]
    depth_x = tile_x // 4
    plane_loads = []
    for part in range(4):
        at = pl.ds(part * depth_x, depth_x)
        plane_loads.append(
            [
                pltpu.make_async_copy(
                    pulses_hbm.at[:, at], result.at[:, at], load_sem.at[0, part]
                ),
                pltpu.make_async_copy(loss_hbm.at[at], loss.at[at], load_sem.at[1, part]),
            ]
        )
    slot_loads = [
        pltpu.make_async_copy(cells_hbm, cells, load_sem.at[2, 0]),
        pltpu.make_async_copy(codes_hbm, codes, load_sem.at[2, 1]),
    ]
    for copy in sum(plane_loads, []) + slot_loads:
        copy.start()
    half_y = size_y // 2
    gx = lax.axis_index("gx")
    gy = lax.axis_index("gy")
    pair, core = gy // 2, gy % 2
    mesh_ids = pl.DeviceIdType.MESH
    arrives = (gx < size_x - 1, gx > 0, gy < size_y - 1, gy > 0)
    leaves = (gx > 0, gx < size_x - 1, gy > 0, gy < size_y - 1)

    barrier = pltpu.get_barrier_semaphore()

    def greet(x, y):
        pl.semaphore_signal(barrier, inc=1, device_id=(x, y), device_id_type=mesh_ids)

    for o in range(1, half_y):
        greet(gx, 2 * ((pair + o) % half_y) + core)
    for o in range(1, size_x):
        greet((gx + o) % size_x, gy)
    greet(gx, 2 * pair + 1 - core)
    other = gy + 2 * core - 1
    has_other = (other >= 0) & (other < size_y)

    @pl.when(has_other)
    def _():
        greet(gx, other)

    row = lax.broadcasted_iota(jnp.int32, (tile_y, tile_z), 0)
    lane = lax.broadcasted_iota(jnp.int32, (tile_y, tile_z), 1)

    def halo_copy(t, kind):
        if kind == 0:
            source, target = refl.at[t, pl.ds(2, 2), 1], refl.at[t, pl.ds(2, 2), tile_x + 1]
            place = (gx - 1, gy)
        elif kind == 1:
            source, target = refl.at[t, pl.ds(0, 2), tile_x], refl.at[t, pl.ds(0, 2), 0]
            place = (gx + 1, gy)
        else:
            source, target = y_face.at[t, kind - 2], y_halo.at[t, kind - 2]
            place = (gx, gy - 1 if kind == 2 else gy + 1)
        return pltpu.make_async_remote_copy(
            src_ref=source,
            dst_ref=target,
            send_sem=halo_send.at[t, kind],
            recv_sem=halo_recv.at[t, kind],
            device_id=place,
            device_id_type=mesh_ids,
        )

    def send_halos(t):
        for kind in range(4):
            @pl.when(leaves[kind])
            def _():
                halo_copy(t, kind).start()

    def await_halos(t):
        for kind in range(4):
            @pl.when(arrives[kind])
            def _():
                halo_copy(t, kind).wait_recv()

            @pl.when(jnp.logical_not(arrives[kind]))
            def _():
                zeros = jnp.zeros((2, tile_y, tile_z), jnp.float32)
                if kind == 0:
                    refl[t, 2:4, tile_x + 1] = zeros
                elif kind == 1:
                    refl[t, 0:2, 0] = zeros
                else:
                    y_halo[t, kind - 2] = jnp.zeros((2, tile_x, tile_z), jnp.float32)

    def keep_reflected(t, x, reflected):
        for k in range(12):
            refl[t, k, x + 1] = reflected[k]
        for k in range(2):
            y_face[t, 0, k, pl.ds(x, 1), :] = reflected[6 + k][0:1]
            y_face[t, 1, k, pl.ds(x, 1), :] = reflected[4 + k][tile_y - 1 : tile_y]

    def incident_at(t, x):
        ports = [None] * 12
        for k in range(2):
            ports[k] = refl[t, 2 + k, x + 2]
            ports[2 + k] = refl[t, k, x]
            after = y_halo[t, 0, k, pl.ds(x, 1), :]
            before = y_halo[t, 1, k, pl.ds(x, 1), :]
            ports[4 + k] = jnp.where(
                row == tile_y - 1, after, pltpu.roll(refl[t, 6 + k, x + 1], tile_y - 1, 0)
            )
            ports[6 + k] = jnp.where(row == 0, before, pltpu.roll(refl[t, 4 + k, x + 1], 1, 0))
            ports[8 + k] = jnp.where(
                lane == tile_z - 1, 0.0, pltpu.roll(refl[t, 10 + k, x + 1], tile_z - 1, 1)
            )
            ports[10 + k] = jnp.where(lane == 0, 0.0, pltpu.roll(refl[t, 8 + k, x + 1], 1, 1))
        return ports

    def keep_fields(x, total, change):
        for c, value in enumerate(node_fields(total, change)):
            high, low = split_two(value)
            at = pl.ds(pl.multiple_of(x * tile_y, 16), tile_y)
            fields[0, c, at, :] = high
            fields[1, c, at, :] = low

    def first_step(x, carry):
        total, change = sums_and_differences([result[k, x] for k in range(12)])
        keep_reflected(0, x, reflect(total, change, 0.5 * loss[x]))
        return carry

    def second_step(x, carry):
        total, change = sums_and_differences(incident_at(0, x))
        keep_fields(x, total, change)
        keep_reflected(1, x, reflect(total, change, 0.5 * loss[x]))
        return carry

    def last_connection(x, carry):
        ports = incident_at(1, x)
        for k in range(12):
            result[k, x] = ports[k]
        total, change = sums_and_differences(ports)
        keep_fields(x, total, change)
        return carry

    for copy in slot_loads:
        copy.wait()
    cell = cells[0]
    code = codes[0]
    column = cell // tile_z
    depth = cell % tile_z
    live = code > 0
    axis_of = (code - 1) // 2
    outward = 1.0 - 2.0 * ((code - 1) % 2).astype(jnp.float32)
    normal = [jnp.where(live & (axis_of == k), outward, 0.0) for k in range(3)]

    def pick(c, carry):
        chosen = jnp.dot(fields[0, c], select_z[...], preferred_element_type=jnp.float32)
        chosen += jnp.dot(fields[1, c], select_z[...], preferred_element_type=jnp.float32)
        rows_of = lax.broadcasted_iota(jnp.int32, chosen.shape, 0)
        picked[c] = jnp.sum(jnp.where(rows_of == column, chosen, 0.0), axis=0, keepdims=True)
        return carry

    def keep_currents(gat, extra):
        lax.fori_loop(0, 6, pick, 0)
        electric = [picked[c] for c in range(3)]
        magnetic = [picked[3 + c] for c in range(3)]
        rows = []
        for sign, vector in ((1.0, magnetic), (-1.0, electric)):
            for k in range(3):
                a, b = (k + 1) % 3, (k + 2) % 3
                rows.append(sign * (normal[a] * vector[b] - normal[b] * vector[a]))
        gat[gx, core, pair] = jnp.concatenate(rows + extra, axis=0)

    def gather_copies(t, phase):
        gat = (gat_one, gat_two)[t]
        if phase == 0:
            count, block, sends, recvs = half_y, gat.at[gx, core, pair], send_z, recv_z
            place = lambda o: (gx, 2 * ((pair + o) % half_y) + core)
        elif phase == 1:
            count, block, sends, recvs = size_x, gat.at[gx, core], send_x, recv_x
            place = lambda o: ((gx + o) % size_x, gy)
        else:
            count, block, sends, recvs = 2, gat.at[pl.ds(0, size_x), core], send_c, recv_c
            place = lambda o: (gx, 2 * pair + 1 - core)
        return [
            pltpu.make_async_remote_copy(
                src_ref=block,
                dst_ref=block,
                send_sem=sends.at[t, o],
                recv_sem=recvs.at[t, o],
                device_id=place(o),
                device_id_type=mesh_ids,
            )
            for o in range(1, count)
        ]

    def begin(t, phase):
        for copy in gather_copies(t, phase):
            copy.start()

    def finish(t, phase):
        for copy in gather_copies(t, phase):
            copy.wait()

    for part, copy in enumerate(plane_loads):
        for landing in copy:
            landing.wait()
        lax.fori_loop(part * depth_x, (part + 1) * depth_x, first_step, 0)
    pl.semaphore_wait(barrier, half_y + size_x - 1 + has_other.astype(jnp.int32))
    send_halos(0)
    depths = lax.broadcasted_iota(jnp.int32, (tile_z, slots), 0)
    select_z[...] = jnp.where(depths == depth, 1.0, 0.0).astype(jnp.bfloat16)
    await_halos(0)
    lax.fori_loop(0, tile_x, second_step, 0)
    send_halos(1)
    x_place = (gx * tile_x + column // tile_y).astype(jnp.float32) - (tile_x * size_x - 1) / 2.0
    y_place = (gy * tile_y + column % tile_y).astype(jnp.float32) - (tile_y * size_y - 1) / 2.0
    keep_currents(gat_one, [x_place, y_place])
    begin(0, 0)
    await_halos(1)
    lax.fori_loop(0, tile_x, last_connection, 0)
    out_copy = pltpu.make_async_copy(result, pulses_out, out_sem)
    out_copy.start()
    finish(0, 0)
    begin(0, 1)
    z_place = depth.astype(jnp.float32) - (tile_z - 1) / 2.0
    keep_currents(gat_two, [z_place, live.astype(jnp.float32)])
    begin(1, 0)
    finish(0, 1)
    begin(0, 2)
    finish(1, 0)
    begin(1, 1)
    finish(0, 2)
    finish(1, 1)
    begin(1, 2)
    for t in range(2):
        for kind in range(4):
            @pl.when(leaves[kind])
            def _():
                halo_copy(t, kind).wait_send()
    out_copy.wait()
    finish(1, 2)


def tlm_and_slots(pulses_in, node_loss, surface_cells, surface_normal):
    size_x, size_y = lax.axis_size("gx"), lax.axis_size("gy")
    tile_x, tile_y, tile_z = node_loss.shape
    slots = surface_cells.shape[2]
    vmem = pl.BlockSpec(memory_space=pltpu.VMEM)
    gat = jax.ShapeDtypeStruct((size_x, 2, size_y // 2, 8, slots), jnp.float32)
    dma = pltpu.SemaphoreType.DMA
    return pl.pallas_call(
        functools.partial(tlm_kernel, size_x, size_y),
        out_shape=(jax.ShapeDtypeStruct(pulses_in.shape, jnp.float32), gat, gat),
        in_specs=[pl.BlockSpec(memory_space=pltpu.HBM)] * 4,
        out_specs=(pl.BlockSpec(memory_space=pltpu.HBM), vmem, vmem),
        scratch_shapes=[
            pltpu.VMEM((2, 12, tile_x + 2, tile_y, tile_z), jnp.float32),
            pltpu.VMEM((2, 2, 2, tile_x, tile_z), jnp.float32),
            pltpu.VMEM((2, 2, 2, tile_x, tile_z), jnp.float32),
            pltpu.VMEM(pulses_in.shape, jnp.float32),
            pltpu.VMEM((2, 6, tile_x * tile_y, tile_z), jnp.bfloat16),
            pltpu.VMEM((tile_z, slots), jnp.bfloat16),
            pltpu.VMEM((6, 1, slots), jnp.float32),
            pltpu.VMEM(node_loss.shape, jnp.float32),
            pltpu.VMEM(surface_cells.shape, jnp.int32),
            pltpu.VMEM(surface_normal.shape, jnp.int32),
            dma((3, 4)),
            dma((2, 4)),
            dma((2, 4)),
            dma((2, size_y // 2)),
            dma((2, size_y // 2)),
            dma((2, size_x)),
            dma((2, size_x)),
            dma((2, 2)),
            dma((2, 2)),
            dma,
        ],
        compiler_params=pltpu.CompilerParams(
            collective_id=0, has_side_effects=True, vmem_limit_bytes=48 * 1024 * 1024
        ),
    )(pulses_in, node_loss, surface_cells, surface_normal)


def trig_coefficients():
    nodes = np.cos(np.pi * (np.arange(64) + 0.5) / 64)
    square = 0.125 * (nodes + 1.0)
    turn = np.sqrt(square)
    cos_fit = np.polynomial.chebyshev.Chebyshev.fit(
        square, np.cos(2 * np.pi * turn), 6, domain=[0.0, 0.25]
    )
    sin_fit = np.polynomial.chebyshev.Chebyshev.fit(
        square, np.sin(2 * np.pi * turn) / turn, 6, domain=[0.0, 0.25]
    )
    to_poly = lambda fit: [float(v) for v in fit.convert(kind=np.polynomial.Polynomial).coef]
    return to_poly(cos_fit), to_poly(sin_fit)


def horner(coefficients, at):
    total = jnp.full_like(at, coefficients[-1])
    for value in coefficients[-2::-1]:
        total = total * at + value
    return total


def cos_sin_turns(turns):
    cos_poly, sin_poly = trig_coefficients()
    rest = turns - jnp.round(turns)
    square = rest * rest
    return horner(cos_poly, square), rest * horner(sin_poly, square)


def split_two(values):
    high = values.astype(jnp.bfloat16)
    low = (values - high.astype(jnp.float32)).astype(jnp.bfloat16)
    return high, low


def output_weights(scale):
    weights = np.zeros((FREQ, 2, 2, 16, FREQ * 12))
    for f in range(FREQ):
        for t in (1, 2):
            w = 2.0 * math.pi * (f + 1) / 64.0 * t
            for c in range(6):
                row = 8 * (t - 1) + c
                weights[f, 0, :, row, 12 * f + c] = math.cos(w)
                weights[f, 1, :, row, 12 * f + c] = math.sin(w)
                weights[f, 0, :, row, 12 * f + 6 + c] = -math.sin(w)
                weights[f, 1, :, row, 12 * f + 6 + c] = math.cos(w)
    weights = (weights * scale).reshape(2 * FREQ, 32, 12 * FREQ)
    return weights.transpose(0, 2, 1).astype(np.float32)


CHUNK = 512
GROUP = 128


def far_kernel(
    pulses, gat_one, gat_two, dirs, weights, pulses_out, out, packed, totals, counts_v, counts_s, sem, pulse_sem
):
    devices, _, slots = gat_one.shape
    rows = dirs.shape[1]
    pulse_copy = pltpu.make_async_copy(pulses, pulses_out, pulse_sem)
    pulse_copy.start()
    flags = gat_two[:, 7, :]
    live = jnp.sum(flags, axis=1, keepdims=True).astype(jnp.int32)
    counts_v[...] = jnp.broadcast_to(live, counts_v.shape)
    copy = pltpu.make_async_copy(counts_v, counts_s, sem)
    copy.start()

    ids = dirs[...]
    theta = (ids // 64).astype(jnp.float32) * (1.0 / 128.0) + 1.0 / 256.0
    azimuth = (ids % 64).astype(jnp.float32) * (1.0 / 64.0)
    cos_t, sin_t = cos_sin_turns(theta)
    cos_a, sin_a = cos_sin_turns(azimuth)
    units = jnp.concatenate([sin_t * cos_a, sin_t * sin_a, cos_t], axis=0) * (1.0 / 32.0)
    first = units.astype(jnp.bfloat16).astype(jnp.float32)
    second = (units - first).astype(jnp.bfloat16).astype(jnp.float32)
    third = units - first - second
    stack = jnp.concatenate(
        [first, second, third, first, second, jnp.zeros((1, rows), jnp.float32)], axis=0
    )
    unit_rows = stack.astype(jnp.bfloat16)
    totals[...] = jnp.zeros_like(totals)
    copy.wait()

    lane = lax.broadcasted_iota(jnp.int32, (16, 128), 1)
    pad = jnp.zeros((16, 128), jnp.float32)

    def pack(d, offset):
        base = pl.multiple_of((offset >> 7) << 7, 128)
        shift = offset & 127
        block = pltpu.roll(jnp.concatenate([jnp.concatenate([gat_one[d], gat_two[d]], axis=0), pad], axis=1), shift, 1)
        packed[:, pl.ds(base, 128)] = jnp.where(
            lane < shift, packed[:, pl.ds(base, 128)], block[:, :128]
        )
        packed[:, pl.ds(base + 128, slots)] = block[:, 128:]
        packed[:, pl.ds(base + 128 + slots, CHUNK)] = jnp.zeros((16, CHUNK), jnp.float32)
        return offset + counts_s[d, 0]

    total = lax.fori_loop(0, devices, pack, jnp.int32(0))

    def chunk_step(index, carry):
        block = packed[:, pl.ds(pl.multiple_of(index * CHUNK, CHUNK), CHUNK)]
        high, low = split_two(block)
        currents = jnp.concatenate([high, low], axis=0)
        twice = jnp.concatenate([currents, currents], axis=1)
        place = jnp.concatenate([block[6:8], block[14:15]], axis=0)
        place_high = place.astype(jnp.bfloat16).astype(jnp.float32)
        place_low = place - place_high
        places = jnp.concatenate(
            [place_high] * 3 + [place_low] * 2 + [jnp.zeros((1, CHUNK), jnp.float32)], axis=0
        ).astype(jnp.bfloat16)
        turns = lax.dot_general(
            places, unit_rows, (((0,), (0,)), ((), ())), preferred_element_type=jnp.float32
        )
        product = jnp.zeros(totals.shape, jnp.float32)
        for g in range(CHUNK // GROUP):
            cos_one, sin_one = cos_sin_turns(turns[g * GROUP : (g + 1) * GROUP])
            double = 2.0 * cos_one
            cos_old, sin_old = jnp.ones_like(cos_one), jnp.zeros_like(sin_one)
            cos_now, sin_now = cos_one, sin_one
            highs, lows = [], []
            for f in range(FREQ):
                for value in (cos_now, sin_now):
                    upper, lower = split_two(value)
                    highs.append(upper)
                    lows.append(lower)
                if f < FREQ - 1:
                    cos_now, cos_old = double * cos_now - cos_old, cos_now
                    sin_now, sin_old = double * sin_now - sin_old, sin_now
            both = jnp.concatenate(
                [jnp.concatenate(highs, axis=1), jnp.concatenate(lows, axis=1)], axis=0
            )
            own = currents[:, g * GROUP : (g + 1) * GROUP]
            product += jnp.dot(
                jnp.concatenate([own, own], axis=1), both, preferred_element_type=jnp.float32
            )
        totals[...] += product
        return carry

    lax.fori_loop(0, (total + CHUNK - 1) // CHUNK, chunk_step, 0)

    result = jnp.zeros((12 * FREQ, rows), jnp.float32)
    for k in range(2 * FREQ):
        result += jnp.dot(
            weights[k],
            totals[:, k * rows : (k + 1) * rows],
            precision=HIGH,
            preferred_element_type=jnp.float32,
        )
    out[...] = result
    pulse_copy.wait()


def far_field_of(pulses, gat_one, gat_two, own_dirs, scale):
    devices, _, slots = gat_one.shape
    rows = own_dirs.shape[1]
    vmem = pl.BlockSpec(memory_space=pltpu.VMEM)
    return pl.pallas_call(
        far_kernel,
        out_shape=(
            jax.ShapeDtypeStruct(pulses.shape, jnp.float32),
            jax.ShapeDtypeStruct((12 * FREQ, rows), jnp.float32),
        ),
        in_specs=[pl.BlockSpec(memory_space=pltpu.HBM)] + [vmem] * 4,
        out_specs=(pl.BlockSpec(memory_space=pltpu.HBM), vmem),
        scratch_shapes=[
            pltpu.VMEM((16, devices * slots + 128 + CHUNK), jnp.float32),
            pltpu.VMEM((32, 2 * FREQ * rows), jnp.float32),
            pltpu.VMEM((devices, 128), jnp.int32),
            pltpu.SMEM((devices, 128), jnp.int32),
            pltpu.SemaphoreType.DMA,
            pltpu.SemaphoreType.DMA,
        ],
        compiler_params=pltpu.CompilerParams(vmem_limit_bytes=48 * 1024 * 1024),
    )(pulses, gat_one, gat_two, own_dirs, jnp.asarray(output_weights(scale)))


def per_device(pulses_in, node_loss, surface_cells, surface_normal, owner_dirs):
    slot_count = surface_cells.shape[2]
    size_x = lax.axis_size("gx")
    size_y = lax.axis_size("gy")
    devices = size_x * size_y
    rows = owner_dirs.shape[0] // devices
    own = lax.axis_index("gx") * size_y + lax.axis_index("gy")
    own_dirs = lax.dynamic_slice(owner_dirs, (own * rows,), (rows,))[None]
    pulses_out, gat_one, gat_two = tlm_and_slots(
        pulses_in, node_loss, surface_cells, surface_normal
    )
    pulses_out, far_field = far_field_of(
        pulses_out,
        gat_one.reshape(devices, 8, slot_count),
        gat_two.reshape(devices, 8, slot_count),
        own_dirs,
        1.0 / math.sqrt(devices * slot_count),
    )
    return (pulses_out, far_field.T)


def solution(mesh):
    return jax.shard_map(
        per_device,
        mesh=mesh,
        in_specs=(
            P(None, "gx", "gy", None),
            P("gx", "gy", None),
            P("gx", "gy", None),
            P("gx", "gy", None),
            P(),
        ),
        out_specs=(P(None, "gx", "gy", None), P(("gx", "gy"), None)),
        check_vma=False,
    )
```

profile of v0, /device:TPU:0, one launch (start us, length us, event | category | flops | bytes accessed | tf_op | source)
XLA Modules:
  0.0 57.5 jit_solution(15151733028084394398)
XLA Ops:
  0.6 0.0 copy-start
  0.6 0.0 copy-start.1
  0.7 0.7 %copy-done = s32[4096]{0:T(1024)S(1)} copy-done((s32[4096]{0:T(1024)S(1)}, s32[4096]{0:T(1024)}, u32[]{:S(2)}) %copy-start) | copy-done | bytes 16408
  1.4 0.1 dynamic-slice_bitcast_fusion.dirs
  1.4 0.0 copy-start.2
  1.4 0.9 %copy-done.2 = f32[16,16,256]{2,1,0:T(8,128)S(1)} copy-done((f32[16,16,256]{2,1,0:T(8,128)S(1)}, f32[16,16,256]{2,1,0:T(8,128)}, u32[]{:S(2)}) %copy-start.2) | copy-done | bytes 262168
  2.4 0.0 copy-start.3
  2.4 0.7 %copy-done.3 = s32[1,1,512]{2,1,0:T(1,128)S(1)} copy-done((s32[1,1,512]{2,1,0:T(1,128)S(1)}, s32[1,1,512]{2,1,0:T(1,128)}, u32[]{:S(2)}) %copy-start.3) | copy-done | bytes 2072
  3.1 0.0 copy-start.4
  3.1 0.7 %copy-done.4 = s32[1,1,512]{2,1,0:T(1,128)S(1)} copy-done((s32[1,1,512]{2,1,0:T(1,128)S(1)}, s32[1,1,512]{2,1,0:T(1,128)}, u32[]{:S(2)}) %copy-start.4) | copy-done | bytes 2072
  3.7 28.6 %shard_map.77 = (f32[12,16,16,256]{3,2,1,0:T(8,128)S(1)}, f32[4,2,4,8,512]{4,3,2,1,0:T(8,128)S(1)}, f32[4,2,4,8,512]{4,3,2,1,0:T(8,128)S(1)}) custom-call(f32[12,16,16,256]{3,2,1,0:T(8,128)} %pulses_hbm.1, f32[16,16,256]{2,1,0:T(8,128)S(1)} %copy-done.2, s32[1,1,512]{2,1,0:T(1,128)S(1)} %copy-done.3, s32[1,1,512]{2,1,0:T(1,128)S(1)} %copy-done.4), custom_call_target="tpu_custom_call" | custom-call | tf_op jit(solution)/shard_map/pallas_call | solution.py:307
  32.3 0.0 copy-done.1
  32.3 25.2 %shard_map.78 = (f32[12,16,16,256]{3,2,1,0:T(8,128)}, f32[96,128]{1,0:T(8,128)}) custom-call(f32[12,16,16,256]{3,2,1,0:T(8,128)S(1)} %get-tuple-element.7.pulses, f32[32,8,512]{2,1,0:T(8,128)S(1)} %bitcast.5, f32[32,8,512]{2,1,0:T(8,128)S(1)} %bitcast.6, s32[1,128]{1,0:T(1,128)S(1)} %dynamic-slice_bitcast_fusion.dirs, f32[16,96,32]{2,1,0:T(8,128)S(1)} %copy-done.1), custom_call_target="tpu_custom_call" | custom-call | tf_op jit(solution)/shard_map/pallas_call | solution.py:495
Async XLA Ops:
  0.6 0.7 %copy-start = (s32[4096]{0:T(1024)S(1)}, s32[4096]{0:T(1024)}, u32[]{:S(2)}) copy-start(s32[4096]{0:T(1024)} %param.10) | copy-start | bytes 49156
  0.6 31.7 %copy-start.1 = (f32[16,96,32]{2,1,0:T(8,128)S(1)}, f32[16,96,32]{2,1,0:T(8,128)}, u32[]{:S(2)}) copy-start(f32[16,96,32]{2,1,0:T(8,128)} %constant.18.clone.weights) | copy-start | bytes 589828
  1.4 0.9 %copy-start.2 = (f32[16,16,256]{2,1,0:T(8,128)S(1)}, f32[16,16,256]{2,1,0:T(8,128)}, u32[]{:S(2)}) copy-start(f32[16,16,256]{2,1,0:T(8,128)} %loss_hbm.1) | copy-start | bytes 786436
  2.4 0.7 %copy-start.3 = (s32[1,1,512]{2,1,0:T(1,128)S(1)}, s32[1,1,512]{2,1,0:T(1,128)}, u32[]{:S(2)}) copy-start(s32[1,1,512]{2,1,0:T(1,128)} %cells_hbm.1) | copy-start | bytes 6148
  3.1 0.7 %copy-start.4 = (s32[1,1,512]{2,1,0:T(1,128)S(1)}, s32[1,1,512]{2,1,0:T(1,128)}, u32[]{:S(2)}) copy-start(s32[1,1,512]{2,1,0:T(1,128)} %codes_hbm.1) | copy-start | bytes 6148
where the time goes:
time: 57.8 us; the launch traced here: 57.5 us
  Pallas kernels  53.8 us (93%)
  local copies, waits for them, and re-layouts  3.09 us (5%)
  between operations  0.67 us (1%)
    pallas_call x1, Pallas kernels, tlm_and_slots(): pl.pallas_call(functools.partial(tlm_kernel, size_x, size_y), out_shape=(...  28.6 us
    pallas_call x1, Pallas kernels, far_field_of(): pl.pallas_call(far_kernel, out_shape=(jax.ShapeDtypeStruct(pulses.shape,...  25.2 us
    unnamed x10, local copies, waits for them, and re-layouts  3.02 us

commit v1 on v0

--- a/solution.py
+++ b/solution.py
@@ -260,20 +260,20 @@
     for part, copy in enumerate(plane_loads):
         for landing in copy:
             landing.wait()
-        lax.fori_loop(part * depth_x, (part + 1) * depth_x, first_step, 0)
+        lax.fori_loop(part * depth_x, (part + 1) * depth_x, first_step, 0, unroll=2)
     pl.semaphore_wait(barrier, half_y + size_x - 1 + has_other.astype(jnp.int32))
     send_halos(0)
     depths = lax.broadcasted_iota(jnp.int32, (tile_z, slots), 0)
     select_z[...] = jnp.where(depths == depth, 1.0, 0.0).astype(jnp.bfloat16)
     await_halos(0)
-    lax.fori_loop(0, tile_x, second_step, 0)
+    lax.fori_loop(0, tile_x, second_step, 0, unroll=2)
     send_halos(1)
     x_place = (gx * tile_x + column // tile_y).astype(jnp.float32) - (tile_x * size_x - 1) / 2.0
     y_place = (gy * tile_y + column % tile_y).astype(jnp.float32) - (tile_y * size_y - 1) / 2.0
     keep_currents(gat_one, [x_place, y_place])
     begin(0, 0)
     await_halos(1)
-    lax.fori_loop(0, tile_x, last_connection, 0)
+    lax.fori_loop(0, tile_x, last_connection, 0, unroll=2)
     out_copy = pltpu.make_async_copy(result, pulses_out, out_sem)
     out_copy.start()
     finish(0, 0)

time: 57.8 us -> 55.2 us (0.955); the launches traced: 57.5 us -> 55.6 us
  Pallas kernels: 53.8 us -> 51.8 us
    pallas_call x1, Pallas kernels: 25.2 us -> 23.8 us  [far_field_of(): pl.pallas_call(far_kernel, out_shape=(jax.ShapeDtypeStruct(pulses.shape,...]
    pallas_call x1, Pallas kernels: 28.6 us -> 28 us  [tlm_and_slots(): pl.pallas_call(functools.partial(tlm_kernel, size_x, size_y), out_shape=(...]
where the time goes in v1:
time: 55.2 us; the launch traced here: 55.6 us
  Pallas kernels  51.8 us (94%)
  local copies, waits for them, and re-layouts  3.09 us (6%)
  between operations  0.67 us (1%)
    pallas_call x1, Pallas kernels, tlm_and_slots(): pl.pallas_call(functools.partial(tlm_kernel, size_x, size_y), out_shape=(...  28 us
    pallas_call x1, Pallas kernels, far_field_of(): pl.pallas_call(far_kernel, out_shape=(jax.ShapeDtypeStruct(pulses.shape,...  23.8 us
    unnamed x10, local copies, waits for them, and re-layouts  3.02 us

profile of v1, /device:TPU:0, one launch (start us, length us, event | category | flops | bytes accessed | tf_op | source)
XLA Modules:
  0.0 55.6 jit_solution(16869495185589706637)
XLA Ops:
  0.6 0.0 copy-start
  0.6 0.0 copy-start.1
  0.7 0.7 %copy-done = s32[4096]{0:T(1024)S(1)} copy-done((s32[4096]{0:T(1024)S(1)}, s32[4096]{0:T(1024)}, u32[]{:S(2)}) %copy-start) | copy-done | bytes 16408
  1.4 0.1 dynamic-slice_bitcast_fusion.dirs
  1.4 0.0 copy-start.2
  1.4 0.9 %copy-done.2 = f32[16,16,256]{2,1,0:T(8,128)S(1)} copy-done((f32[16,16,256]{2,1,0:T(8,128)S(1)}, f32[16,16,256]{2,1,0:T(8,128)}, u32[]{:S(2)}) %copy-start.2) | copy-done | bytes 262168
  2.4 0.0 copy-start.3
  2.4 0.7 %copy-done.3 = s32[1,1,512]{2,1,0:T(1,128)S(1)} copy-done((s32[1,1,512]{2,1,0:T(1,128)S(1)}, s32[1,1,512]{2,1,0:T(1,128)}, u32[]{:S(2)}) %copy-start.3) | copy-done | bytes 2072
  3.1 0.0 copy-start.4
  3.1 0.7 %copy-done.4 = s32[1,1,512]{2,1,0:T(1,128)S(1)} copy-done((s32[1,1,512]{2,1,0:T(1,128)S(1)}, s32[1,1,512]{2,1,0:T(1,128)}, u32[]{:S(2)}) %copy-start.4) | copy-done | bytes 2072
  3.7 28.0 %shard_map.77 = (f32[12,16,16,256]{3,2,1,0:T(8,128)S(1)}, f32[4,2,4,8,512]{4,3,2,1,0:T(8,128)S(1)}, f32[4,2,4,8,512]{4,3,2,1,0:T(8,128)S(1)}) custom-call(f32[12,16,16,256]{3,2,1,0:T(8,128)} %pulses_hbm.1, f32[16,16,256]{2,1,0:T(8,128)S(1)} %copy-done.2, s32[1,1,512]{2,1,0:T(1,128)S(1)} %copy-done.3, s32[1,1,512]{2,1,0:T(1,128)S(1)} %copy-done.4), custom_call_target="tpu_custom_call" | custom-call | tf_op jit(solution)/shard_map/pallas_call | solution.py:307
  31.8 0.0 copy-done.1
  31.8 23.8 %shard_map.78 = (f32[12,16,16,256]{3,2,1,0:T(8,128)}, f32[96,128]{1,0:T(8,128)}) custom-call(f32[12,16,16,256]{3,2,1,0:T(8,128)S(1)} %get-tuple-element.7.pulses, f32[32,8,512]{2,1,0:T(8,128)S(1)} %bitcast.5, f32[32,8,512]{2,1,0:T(8,128)S(1)} %bitcast.6, s32[1,128]{1,0:T(1,128)S(1)} %dynamic-slice_bitcast_fusion.dirs, f32[16,96,32]{2,1,0:T(8,128)S(1)} %copy-done.1), custom_call_target="tpu_custom_call" | custom-call | tf_op jit(solution)/shard_map/pallas_call | solution.py:495
Async XLA Ops:
  0.6 0.7 %copy-start = (s32[4096]{0:T(1024)S(1)}, s32[4096]{0:T(1024)}, u32[]{:S(2)}) copy-start(s32[4096]{0:T(1024)} %param.10) | copy-start | bytes 49156
  0.6 31.1 %copy-start.1 = (f32[16,96,32]{2,1,0:T(8,128)S(1)}, f32[16,96,32]{2,1,0:T(8,128)}, u32[]{:S(2)}) copy-start(f32[16,96,32]{2,1,0:T(8,128)} %constant.18.clone.weights) | copy-start | bytes 589828
  1.4 0.9 %copy-start.2 = (f32[16,16,256]{2,1,0:T(8,128)S(1)}, f32[16,16,256]{2,1,0:T(8,128)}, u32[]{:S(2)}) copy-start(f32[16,16,256]{2,1,0:T(8,128)} %loss_hbm.1) | copy-start | bytes 786436
  2.4 0.7 %copy-start.3 = (s32[1,1,512]{2,1,0:T(1,128)S(1)}, s32[1,1,512]{2,1,0:T(1,128)}, u32[]{:S(2)}) copy-start(s32[1,1,512]{2,1,0:T(1,128)} %cells_hbm.1) | copy-start | bytes 6148
  3.1 0.7 %copy-start.4 = (s32[1,1,512]{2,1,0:T(1,128)S(1)}, s32[1,1,512]{2,1,0:T(1,128)}, u32[]{:S(2)}) copy-start(s32[1,1,512]{2,1,0:T(1,128)} %codes_hbm.1) | copy-start | bytes 6148
